TPU v7x, 32 devices: a whole 2x2x4 slice. The times are simulated.
32 devices in a mesh: groups: 2 (over y), rows: 4 (over z), cols: 2 (over x), chan: 2 (over core).
Axes of the slice: x: 2, y: 2, z: 4, core: 2. Of those that a mesh axis runs over, the one named last changes fastest.
Arguments:
- patches: bfloat16 [128, 16, 1024], P(('groups', 'rows'), 'cols', 'chan'), parts along dimension 0, may hold values from -6 to 6
- steps: float32 [128, 16, 1024], P(('groups', 'rows'), 'cols', 'chan'), parts along dimension 0, may hold values from 0.1 to 1
- decay_codes: int32 [128, 16], P(('groups', 'rows'), 'cols'), parts along dimension 0, may hold values from 0 to 15
- tissue_mask: int32 [128, 16], P(('groups', 'rows'), 'cols'), parts along dimension 0, may hold values 0 or 1
- decay_rates: float32 [16, 1024], P(None, 'chan'), may hold values from 0.002 to 4
- input_map: float32 [128, 16, 16], P(('groups', 'rows'), 'cols'), parts along dimension 0, may hold values from -1.5 to 1.5
- output_map: float32 [128, 16, 16], P(('groups', 'rows'), 'cols'), parts along dimension 0, may hold values from -1.5 to 1.5
- out_grad: bfloat16 [128, 16, 1024], P(('groups', 'rows'), 'cols', 'chan'), parts along dimension 0, may hold values from -0.59765625 to 0.59765625
Outputs:
- patches_grad: bfloat16 [128, 16, 1024], P(('groups', 'rows'), 'cols', 'chan'), parts along dimension 0
- steps_grad: float32 [128, 16, 1024], P(('groups', 'rows'), 'cols', 'chan'), parts along dimension 0
- input_map_grad: float32 [128, 16, 16], P(('groups', 'rows'), 'cols'), parts along dimension 0
- output_map_grad: float32 [128, 16, 16], P(('groups', 'rows'), 'cols'), parts along dimension 0
There are 2 independent parts, one for each index of `groups`. A program takes and returns all parts, laid end to end along the dimension named above; an argument that names none is the same for every part. Nothing has to cross between parts.
Inputs may be any that keep to these rules, and one draw needn't show every extreme that they name: `decay_codes`: a decay code of each patch.
All inputs are finite; a program needn't handle non-finite values. No bound on the sum of `tissue_mask` on one device may be relied on, other than what follows from the above.
Results may differ from a plain program's by a relative error of at most 0.0014.
Values sent between devices are 32-bit elements; how exact they have to be, the bound alone decides.
A program may use at most 128 MiB of HBM per device.

v0:
```python
import jax
import jax.numpy as jnp
from jax import lax
from jax.sharding import PartitionSpec as P

CODES = 16


def shifted(block, axis, distance):
    devices = range(lax.axis_size(axis))
    route = [(i - distance, i) for i in devices if i - distance in devices]
    return lax.ppermute(block, axis, route)


def relay_carry(factor, offset, sender, count):

    def advance(turn, carry):
        return sender(factor * carry + offset)

    return lax.fori_loop(0, count, advance, jnp.zeros_like(offset))


def local(patches, steps, decay_codes, tissue_mask, decay_rates, input_map, output_map, out_grad):
    prows = steps.shape[0]
    pcols = steps.shape[1]
    maskf = tissue_mask.astype(jnp.float32)
    levels = 0.7 + 0.25 * decay_codes.astype(jnp.float32) / (CODES - 1)
    keep = maskf * jnp.log(levels)
    xf = patches.astype(jnp.float32)
    gyf = out_grad.astype(jnp.float32)
    drive = maskf[:, :, None] * steps * xf
    log_step = keep[:, :, None] * steps
    row_expo = jnp.sum(log_step, axis=1)
    col_expo = jnp.sum(log_step, axis=0)
    row_factor = jnp.exp(row_expo[:, None, :] * decay_rates[None])
    col_factor = jnp.exp(col_expo[:, None, :] * decay_rates[None])
    row_zero = jnp.zeros(row_factor.shape, jnp.float32)
    col_zero = jnp.zeros(col_factor.shape, jnp.float32)

    def decay_of(kept, stepped):
        return jnp.exp(kept[:, None, None] * decay_rates[None] * stepped[:, None, :])

    def row_forward(carry, j):
        factor = decay_of(keep[:, j], steps[:, j])
        carry = factor * carry + input_map[:, j, :, None] * drive[:, j][:, None, :]
        return (carry, carry)

    def row_forward_last(carry, j):
        return (row_forward(carry, j)[0], None)

    row_offset, _ = lax.scan(row_forward_last, row_zero, jnp.arange(pcols))
    left_in = relay_carry(
        row_factor, row_offset, lambda value: shifted(value, "cols", 1), lax.axis_size("cols") - 1
    )
    _, row_state_t = lax.scan(row_forward, left_in, jnp.arange(pcols))

    def col_forward(carry, i):
        factor = decay_of(keep[i], steps[i])
        carry = factor * carry + row_state_t[:, i]
        return (carry, carry)

    def col_forward_last(carry, i):
        return (col_forward(carry, i)[0], None)

    col_offset, _ = lax.scan(col_forward_last, col_zero, jnp.arange(prows))
    top_in = relay_carry(
        col_factor, col_offset, lambda value: shifted(value, "rows", 1), lax.axis_size("rows") - 1
    )

    def col_forward_out(carry, i):
        carry, _ = col_forward(carry, i)
        return (carry, (carry, jnp.sum(gyf[i][:, None, :] * carry, axis=2)))

    _, (state, map_out) = lax.scan(col_forward_out, top_in, jnp.arange(prows))

    def col_backward(carry, i):
        factor = decay_of(keep[i], steps[i])
        cot = output_map[i][:, :, None] * gyf[i][:, None, :] + carry
        return (factor * cot, cot)

    def col_backward_last(carry, i):
        return (col_backward(carry, i)[0], None)

    up_offset, _ = lax.scan(col_backward_last, col_zero, jnp.arange(prows), reverse=True)
    bottom_in = relay_carry(
        col_factor, up_offset, lambda value: shifted(value, "rows", -1), lax.axis_size("rows") - 1
    )
    _, col_cot = lax.scan(col_backward, bottom_in, jnp.arange(prows), reverse=True)

    def row_backward_last(carry, j):
        factor = decay_of(keep[:, j], steps[:, j])
        return (factor * (col_cot[:, j] + carry), None)

    lead_offset, _ = lax.scan(row_backward_last, row_zero, jnp.arange(pcols), reverse=True)
    right_in = relay_carry(
        row_factor, lead_offset, lambda value: shifted(value, "cols", -1), lax.axis_size("cols") - 1
    )

    def row_backward(carry, j):
        kept = keep[:, j]
        stepped = steps[:, j]
        factor = decay_of(kept, stepped)
        col_here = col_cot[:, j]
        row_here = col_here + carry
        state_col = state[:, j]
        above = jnp.concatenate([top_in[j][None], state_col[:-1]], axis=0)
        left = jnp.where(j > 0, row_state_t[jnp.maximum(j - 1, 0)], left_in)
        decay_cot = factor * (col_here * above + row_here * left)
        drive_cot = jnp.sum(row_here * input_map[:, j, :, None], axis=1)
        masked = maskf[:, j][:, None]
        grad_x = (drive_cot * masked * stepped).astype(jnp.bfloat16)
        grad_s = drive_cot * masked * xf[:, j] + jnp.sum(
            decay_cot * kept[:, None, None] * decay_rates[None], axis=1
        )
        grad_in = jnp.sum(row_here * drive[:, j][:, None, :], axis=2)
        return (factor * row_here, (grad_x, grad_s, grad_in))

    _, (grad_x, grad_s, map_in) = lax.scan(row_backward, right_in, jnp.arange(pcols), reverse=True)
    patches_grad = jnp.moveaxis(grad_x, 0, 1)
    steps_grad = jnp.moveaxis(grad_s, 0, 1)
    map_in = jnp.moveaxis(map_in, 0, 1)
    input_grad, output_grad = lax.psum((map_in, map_out), "chan")
    return (patches_grad, steps_grad, input_grad, output_grad)


def solution(mesh):
    in_specs = (
        P(("groups", "rows"), "cols", "chan"),
        P(("groups", "rows"), "cols", "chan"),
        P(("groups", "rows"), "cols"),
        P(("groups", "rows"), "cols"),
        P(None, "chan"),
        P(("groups", "rows"), "cols", None),
        P(("groups", "rows"), "cols", None),
        P(("groups", "rows"), "cols", "chan"),
    )
    out_specs = (
        P(("groups", "rows"), "cols", "chan"),
        P(("groups", "rows"), "cols", "chan"),
        P(("groups", "rows"), "cols", None),
        P(("groups", "rows"), "cols", None),
    )
    return jax.shard_map(local, mesh=mesh, in_specs=in_specs, out_specs=out_specs, check_vma=False)
```

profile of v0, /device:TPU:0, one launch (start us, length us, event | category | flops | bytes accessed | tf_op | source)
XLA Modules:
  0.0 537.3 jit_solution(17045311224574142558)
XLA Ops:
  4.3 77.7 %while.151 = (s32[]{:T(128)}, f32[8,16,512]{2,1,0:T(8,128)S(1)}, s32[16]{0:T(128)S(1)}, f32[16,8]{1,0:T(8,128)S(1)}, f32[16,512]{1,0:T(8,128)}, /*index=5*/f32[1...) while((s32[]{:T(128)}, f32[8,16,512]{2,1,0:T(8,128)S(1)}, ...), condition=%wide.region_3.4_spmd.clone, body=%wide.region_2.3_spmd.clone.sunk | while | flops 393223 | bytes 657189 | solution.py:84
  82.1 31.6 %while.149 = (s32[]{:T(128)}, f32[8,16,512]{2,1,0:T(8,128)S(1)}, f32[8,16,512]{2,1,0:T(8,128)S(1)}, f32[16,512]{1,0:T(8,128)}, f32[8,512]{1,0:T(8,128)S(1)}, /*index=5*/s32[]{:T(128)}) while((s32[]{:T(128)}, f32[8,16,512]{2,1,0:T(8,128)S(1)}, f32[8,16,512]{2,1,0:T(8,128)S(1)}, f32[16,512]{1,0:T(8,128)}, f32[8,512]{1,0:T(8,128)S(1)}, ...), condition=%wide.region_5.6_spmd.clone, body=%wide.region_4.5_spmd.clone.sunk | while | flops 196610 | bytes 1884269 | solution.py:20
  83.0 1.3 collective-permute-start
  84.3 9.9 %collective-permute-done = f32[8,16,512]{2,1,0:T(8,128)S(1)} collective-permute-done((f32[8,16,512]{2,1,0:T(8,128)S(1)}, f32[8,16,512]{2,1,0:T(8,128)S(1)}, u32[]{:S(2)}, u32[]{:S(2)}) %collective-permute-start) | collective-permute-done | bytes 262176 | tf_op jit(solution)/shard_map/while/body/eval_jaxpr/ppermute | solution.py:12
  95.0 1.3 collective-permute-start
  96.3 8.1 %collective-permute-done = f32[8,16,512]{2,1,0:T(8,128)S(1)} collective-permute-done((f32[8,16,512]{2,1,0:T(8,128)S(1)}, f32[8,16,512]{2,1,0:T(8,128)S(1)}, u32[]{:S(2)}, u32[]{:S(2)}) %collective-permute-start) | collective-permute-done | bytes 262176 | tf_op jit(solution)/shard_map/while/body/eval_jaxpr/ppermute | solution.py:12
  105.2 1.3 collective-permute-start
  106.5 7.2 %collective-permute-done = f32[8,16,512]{2,1,0:T(8,128)S(1)} collective-permute-done((f32[8,16,512]{2,1,0:T(8,128)S(1)}, f32[8,16,512]{2,1,0:T(8,128)S(1)}, u32[]{:S(2)}, u32[]{:S(2)}) %collective-permute-start) | collective-permute-done | bytes 262176 | tf_op jit(solution)/shard_map/while/body/eval_jaxpr/ppermute | solution.py:12
  113.7 2.5 broadcast.67.clone
  116.1 68.1 %while.145 = (s32[]{:T(128)}, f32[8,16,512]{2,1,0:T(8,128)S(1)}, f32[16,8,16,512]{3,2,0,1:T(8,128)}, s32[16]{0:T(128)S(1)}, f32[16,8]{1,0:T(8,128)S(1)}, /*index...) while((s32[]{:T(128)}, f32[8,16,512]{2,1,0:T(8,128)S(1)}, ...), condition=%wide.region_7.8_spmd, body=%wide.region_6.7_spmd.sunk | while | flops 458758 | bytes 1198375 | solution.py:88
  184.5 30.8 %while.152 = (s32[]{:T(128)}, f32[16,16,512]{2,1,0:T(8,128)S(1)}, s32[8]{0:T(128)S(1)}, f32[16,8]{0,1:T(8,128)S(1)}, f32[16,512]{1,0:T(8,128)S(1)}, /*index=5*/f...) while((s32[]{:T(128)}, f32[16,16,512]{2,1,0:T(8,128)S(1)}, ...), condition=%wide.region_9.10_spmd.clone, body=%wide.region_8.9_spmd.clone.sunk | while | flops 655367 | bytes 1704317 | solution.py:94
  215.4 23.4 %while.153 = (s32[]{:T(128)}, f32[16,16,512]{2,1,0:T(8,128)S(1)}, s32[8]{0:T(128)S(1)}, f32[16,8]{0,1:T(8,128)S(1)}, f32[16,512]{1,0:T(8,128)S(1)}, /*index=5*/f...) while((s32[]{:T(128)}, f32[16,16,512]{2,1,0:T(8,128)S(1)}, ...), condition=%wide.region_11.12_spmd.clone, body=%wide.region_10.11_spmd.clone.sunk | while | flops 786438 | bytes 1281393 | solution.py:51
  239.8 3.1 collective-permute-start.3
  242.8 1.3 collective-permute-start.2
  244.2 6.8 %collective-permute-done.3 = f32[16,16,512]{2,1,0:T(8,128)S(1)} collective-permute-done((f32[16,16,512]{2,1,0:T(8,128)S(1)}, f32[16,16,512]{2,1,0:T(8,128)S(1)}, u32[]{:S(2)}, u32[]{:S(2)}) %collective-permute-start.3) | collective-permute-done | bytes 524320 | tf_op jit(solution)/shard_map/while/body/eval_jaxpr/ppermute | solution.py:12
  251.1 28.8 %while.146 = (s32[]{:T(128)}, f32[16,16,512]{2,1,0:T(8,128)S(1)}, f32[8,16,16,512]{3,2,1,0:T(8,128)}, s32[8]{0:T(128)S(1)}, f32[16,8]{0,1:T(8,128)S(1)}, /*index...) while((s32[]{:T(128)}, f32[16,16,512]{2,1,0:T(8,128)S(1)}, ...), condition=%wide.region_13.14_spmd, body=%wide.region_12.13_spmd.sunk | while | flops 655365 | bytes 1806191 | solution.py:55
  279.8 5.0 copy.26
  284.8 58.9 %while.154 = (s32[]{:T(128)}, f32[8,16,512]{2,1,0:T(8,128)S(1)}, s32[16]{0:T(128)S(1)}, f32[16,8]{1,0:T(8,128)S(1)}, f32[16,512]{1,0:T(8,128)S(1)}, /*index=5*/f...) while((s32[]{:T(128)}, f32[8,16,512]{2,1,0:T(8,128)S(1)}, ...), condition=%wide.region_15.16_spmd.clone, body=%wide.region_14.15_spmd.clone.sunk | while | flops 327686 | bytes 868617 | solution.py:65
  343.8 26.4 %while.150 = (s32[]{:T(128)}, f32[8,16,512]{2,1,0:T(8,128)S(1)}, f32[8,16,512]{2,1,0:T(8,128)S(1)}, f32[16,512]{1,0:T(8,128)S(1)}, f32[8,512]{1,0:T(8,128)S(1)}, /*index=5*/s32[]{:T(128)}) while((s32[]{:T(128)}, f32[8,16,512]{2,1,0:T(8,128)S(1)}, f32[8,16,512]{2,1,0:T(8,128)S(1)}, f32[16,512]{1,0:T(8,128)S(1)}, ...), condition=%wide.region_17.18_spmd.clone, body=%wide.region_16.17_spmd.clone.sunk | while | flops 196610 | bytes 1884269 | solution.py:20
  343.9 3.5 collective-permute-start.1
  347.4 4.4 collective-permute-done.1
  351.9 4.4 collective-permute-start.1
  356.3 5.6 %collective-permute-done.1 = f32[8,16,512]{2,1,0:T(8,128)S(1)} collective-permute-done((f32[8,16,512]{2,1,0:T(8,128)S(1)}, f32[8,16,512]{2,1,0:T(8,128)S(1)}, u32[]{:S(2)}, u32[]{:S(2)}) %collective-permute-start.1) | collective-permute-done | bytes 262176 | tf_op jit(solution)/shard_map/while/body/eval_jaxpr/ppermute | solution.py:12
  361.9 4.4 collective-permute-start.1
  366.3 3.9 collective-permute-done.1
  370.2 83.3 %while.147 = (s32[]{:T(128)}, f32[8,16,512]{2,1,0:T(8,128)S(1)}, f32[16,8,16,512]{3,2,1,0:T(8,128)}, f32[16,8,16]{2,1,0:T(8,128)}, s32[16]{0:T(128)S(1)}, /*inde...) while((s32[]{:T(128)}, f32[8,16,512]{2,1,0:T(8,128)S(1)}, ...), condition=%wide.region_20.21_spmd, body=%wide.region_18.20_spmd.sunk | while | flops 393093 | bytes 1448215 | solution.py:74
  383.2 1.3 multiply_reduce_fusion.7
  393.6 1.3 multiply_reduce_fusion.7
  404.0 1.3 multiply_reduce_fusion.7
  454.9 75.8 %while.148 = (s32[]{:T(128)}, f32[16,16,512]{2,1,0:T(8,128)S(1)}, bf16[8,16,512]{2,1,0:T(8,128)(2,1)}, f32[8,16,512]{2,0,1:T(8,128)}, f32[8,16,16]{2,0,1:T(8,128...) while((s32[]{:T(128)}, f32[16,16,512]{2,1,0:T(8,128)S(1)}, ...), condition=%wide.region_25.26_spmd, body=%wide.region_21.25_spmd.sunk | while | flops 2522889 | bytes 7002969 | solution.py:118
  459.9 1.7 multiply_reduce_fusion.8
  461.7 1.8 dynamic_update_slice.71
  469.4 1.7 multiply_reduce_fusion.8
  471.2 1.8 dynamic_update_slice.71
  478.8 1.7 multiply_reduce_fusion.8
  480.6 1.8 dynamic_update_slice.71
  488.3 1.7 multiply_reduce_fusion.8
  490.1 1.8 dynamic_update_slice.71
  497.8 1.7 multiply_reduce_fusion.8
  499.6 1.8 dynamic_update_slice.71
  507.3 1.7 multiply_reduce_fusion.8
  509.1 1.8 dynamic_update_slice.71
  516.8 1.7 multiply_reduce_fusion.8
  518.5 1.8 dynamic_update_slice.71
  526.2 1.7 multiply_reduce_fusion.8
  528.0 1.8 dynamic_update_slice.71
  530.7 1.6 copy.52
  532.3 5.0 all-reduce
  (590 shorter events, 227.4 us)
Async XLA Ops:
  82.1 34.1 %copy-start.1 = (f32[16,8,512]{2,1,0:T(8,128)S(1)}, f32[16,8,512]{2,1,0:T(8,128)}, u32[]{:S(2)}) copy-start(f32[16,8,512]{2,1,0:T(8,128)} %get-tuple-element.2470) | copy-start | bytes 786436
  83.0 11.2 %collective-permute-start = (f32[8,16,512]{2,1,0:T(8,128)S(1)}, f32[8,16,512]{2,1,0:T(8,128)S(1)}, u32[]{:S(2)}, u32[]{:S(2)}) collective-permute-start(f32[8,16,512]{2,1,0:T(8,128)S(1)} %fusion.50), channel_id=1, source_target_pairs={{4,0},{8,4},{12,8},{5,1},{9,5},{13,9},{6,2},{10,6},{14,10},{7,3},{... | collective-permute-start | bytes 786440 | tf_op jit(solution)/shard_map/while/body/eval_jaxpr/ppermute | solution.py:12
  95.0 9.4 %collective-permute-start = (f32[8,16,512]{2,1,0:T(8,128)S(1)}, f32[8,16,512]{2,1,0:T(8,128)S(1)}, u32[]{:S(2)}, u32[]{:S(2)}) collective-permute-start(f32[8,16,512]{2,1,0:T(8,128)S(1)} %fusion.50), channel_id=1, source_target_pairs={{4,0},{8,4},{12,8},{5,1},{9,5},{13,9},{6,2},{10,6},{14,10},{7,3},{... | collective-permute-start | bytes 786440 | tf_op jit(solution)/shard_map/while/body/eval_jaxpr/ppermute | solution.py:12
  105.2 8.5 %collective-permute-start = (f32[8,16,512]{2,1,0:T(8,128)S(1)}, f32[8,16,512]{2,1,0:T(8,128)S(1)}, u32[]{:S(2)}, u32[]{:S(2)}) collective-permute-start(f32[8,16,512]{2,1,0:T(8,128)S(1)} %fusion.50), channel_id=1, source_target_pairs={{4,0},{8,4},{12,8},{5,1},{9,5},{13,9},{6,2},{10,6},{14,10},{7,3},{... | collective-permute-start | bytes 786440 | tf_op jit(solution)/shard_map/while/body/eval_jaxpr/ppermute | solution.py:12
  113.7 2.5 copy-start
  116.1 68.2 %copy-start.2 = (bf16[16,8,512]{2,1,0:T(8,128)(2,1)S(1)}, bf16[16,8,512]{2,1,0:T(8,128)(2,1)}, u32[]{:S(2)}) copy-start(bf16[16,8,512]{2,1,0:T(8,128)(2,1)} %param.28) | copy-start | bytes 393220
  184.5 30.8 %copy-start.3 = (f32[16,8,16]{2,1,0:T(8,128)S(1)}, f32[16,8,16]{2,1,0:T(8,128)}, u32[]{:S(2)}) copy-start(f32[16,8,16]{2,1,0:T(8,128)} %param.33) | copy-start | bytes 24580
  239.8 11.3 %collective-permute-start.3 = (f32[16,16,512]{2,1,0:T(8,128)S(1)}, f32[16,16,512]{2,1,0:T(8,128)S(1)}, u32[]{:S(2)}, u32[]{:S(2)}) collective-permute-start(f32[16,16,512]{2,1,0:T(8,128)S(1)} %get-tuple-element.1527), channel_id=1, source_target_pairs={{0,2},{1,3},{4,6},{5,7},{8,10},{9,11},{12,14},{13,15},{16,18},{17,... | collective-permute-start | bytes 1572872 | tf_op jit(solution)/shard_map/while/body/eval_jaxpr/ppermute | solution.py:12
  242.8 210.6 %collective-permute-start.2 = (f32[16,16,512]{2,1,0:T(8,128)}, f32[16,16,512]{2,1,0:T(8,128)S(1)}, u32[]{:S(2)}, u32[]{:S(2)}) collective-permute-start(f32[16,16,512]{2,1,0:T(8,128)} %get-tuple-element.1528), channel_id=1, source_target_pairs={{2,0},{3,1},{6,4},{7,5},{10,8},{11,9},{14,12},{15,13},{18,16},{19,... | collective-permute-start | bytes 1572872 | tf_op jit(solution)/shard_map/while/body/eval_jaxpr/ppermute | solution.py:12
  343.9 7.9 %collective-permute-start.1 = (f32[8,16,512]{2,1,0:T(8,128)S(1)}, f32[8,16,512]{2,1,0:T(8,128)S(1)}, u32[]{:S(2)}, u32[]{:S(2)}) collective-permute-start(f32[8,16,512]{2,1,0:T(8,128)S(1)} %fusion.51), channel_id=1, source_target_pairs={{0,4},{4,8},{8,12},{1,5},{5,9},{9,13},{2,6},{6,10},{10,14},{3,7},{... | collective-permute-start | bytes 786440 | tf_op jit(solution)/shard_map/while/body/eval_jaxpr/ppermute | solution.py:12
  351.9 10.0 %collective-permute-start.1 = (f32[8,16,512]{2,1,0:T(8,128)S(1)}, f32[8,16,512]{2,1,0:T(8,128)S(1)}, u32[]{:S(2)}, u32[]{:S(2)}) collective-permute-start(f32[8,16,512]{2,1,0:T(8,128)S(1)} %fusion.51), channel_id=1, source_target_pairs={{0,4},{4,8},{8,12},{1,5},{5,9},{9,13},{2,6},{6,10},{10,14},{3,7},{... | collective-permute-start | bytes 786440 | tf_op jit(solution)/shard_map/while/body/eval_jaxpr/ppermute | solution.py:12
  361.9 8.3 %collective-permute-start.1 = (f32[8,16,512]{2,1,0:T(8,128)S(1)}, f32[8,16,512]{2,1,0:T(8,128)S(1)}, u32[]{:S(2)}, u32[]{:S(2)}) collective-permute-start(f32[8,16,512]{2,1,0:T(8,128)S(1)} %fusion.51), channel_id=1, source_target_pairs={{0,4},{4,8},{8,12},{1,5},{5,9},{9,13},{2,6},{6,10},{10,14},{3,7},{... | collective-permute-start | bytes 786440 | tf_op jit(solution)/shard_map/while/body/eval_jaxpr/ppermute | solution.py:12
where the time goes:
time: 547 us; the launch traced here: 537 us
  loops' own time  197 us (36%)
  local copies, waits for them, and re-layouts  151 us (28%)
  other arithmetic  117 us (21%)
  waiting for transfers between devices  45.8 us (8%)
  starting transfers between devices  20.5 us (4%)
    ppermute x8, waiting for transfers between devices, shifted(): return lax.ppermute(block, axis, route)  45.8 us
    dynamic_slice x64, local copies, waits for them, and re-layouts, local(): col_offset, _ = lax.scan(col_forward_last, col_zero, jnp.arange(prows))  38.5 us
    mul x64, local copies, waits for them, and re-layouts, col_backward(): cot = output_map[i][:, :, None] * gyf[i][:, None, :] + carry  33.9 us
    another operation x1, loops' own time, local(): col_offset, _ = lax.scan(col_forward_last, col_zero, jnp.arange(prows))  31.7 us
    another operation x1, loops' own time, local(): lax.scan(col_backward, bottom_in, jnp.arange(prows), reverse=True)  31.6 us
    another operation x1, loops' own time, local(): _, (state, map_out) = lax.scan(col_forward_out, top_in, jnp.arange(prows))  31.4 us
    another operation x1, loops' own time, local(): lax.scan(col_backward_last, col_zero, jnp.arange(prows), reverse=True)  30.3 us
    another operation x1, loops' own time, local(): lax.scan(row_backward, right_in, jnp.arange(pcols), reverse=True)  26.6 us
  transfers between devices with their start and end apart: 8, of which 7 were waited for; matrix products, arithmetic and copies ran while one was open for 18% of the time, Pallas kernels for 0%

commit v1 on v0

v1 whole, which is shorter than its diff:
```python
import functools

import jax
import jax.numpy as jnp
from jax import lax
from jax.experimental import pallas as pl
from jax.experimental.pallas import tpu as pltpu
from jax.sharding import PartitionSpec as P

CODES = 16
LANES = 128
F32 = jnp.float32
RIGHT, DOWN, UP, LEFT = range(4)


def kernel(dims, x_ref, steps_ref, codes_ref, mask_ref, rates_ref, imap_ref, omap_ref, gy_ref,
           gx_ref, gs_ref, sums_ref,
           im, om, kb, mb, lt, dr, gy, cs, decay, rst, cct,
           right_off, left_in, down_off, top_in, up_off, bottom_in, left_off, right_in,
           acc_in, acc_out, dc_rows, ds_rows, mine, theirs,
           send_sem, recv_sem, pair_send, pair_recv):
    rows, cols, chans, ni, nj, ns, chunks = dims
    row, col, chan = lax.axis_index("rows"), lax.axis_index("cols"), lax.axis_index("chan")
    peer = lax.rem(chan + 1, chans)
    first_row, last_row = row == 0, row == rows - 1
    first_col, last_col = col == 0, col == cols - 1

    barrier = pltpu.get_barrier_semaphore()

    def greet(there, target):
        @pl.when(there)
        def _():
            pl.semaphore_signal(barrier, inc=1, device_id=target, device_id_type=pl.DeviceIdType.MESH)

    greet(jnp.logical_not(first_row), {"rows": row - 1})
    greet(jnp.logical_not(last_row), {"rows": row + 1})
    greet(jnp.logical_not(first_col), {"cols": col - 1})
    greet(jnp.logical_not(last_col), {"cols": col + 1})
    pl.semaphore_signal(barrier, inc=1, device_id={"chan": peer}, device_id_type=pl.DeviceIdType.MESH)

    patches = ni * nj

    def turned(value, size):
        one = (lax.broadcasted_iota(jnp.int32, (size, size), 0)
               == lax.broadcasted_iota(jnp.int32, (size, size), 1)).astype(F32)
        return lax.dot_general(one, value, (((1,), (1,)), ((), ())),
                               precision=lax.Precision.HIGHEST, preferred_element_type=F32)

    maskf = mask_ref[...].astype(F32)
    keep = maskf * jnp.log(0.7 + 0.25 * codes_ref[...].astype(F32) / (CODES - 1))
    keep_t, mask_t = turned(keep, nj), turned(maskf, nj)
    for i in range(ni):
        kb[i] = jnp.broadcast_to(keep_t[:, i:i + 1], (nj, LANES))
        mb[i] = jnp.broadcast_to(mask_t[:, i:i + 1], (nj, LANES))
    im_t, om_t = turned(imap_ref[...], ns), turned(omap_ref[...], ns)
    for p in range(patches):
        im[p // nj, p % nj] = jnp.broadcast_to(im_t[:, p:p + 1], (ns, LANES))
        om[p // nj, p % nj] = jnp.broadcast_to(om_t[:, p:p + 1], (ns, LANES))

    @pl.when(first_col)
    def _():
        left_in[...] = jnp.zeros_like(left_in)

    @pl.when(last_col)
    def _():
        right_in[...] = jnp.zeros_like(right_in)

    @pl.when(first_row)
    def _():
        top_in[...] = jnp.zeros_like(top_in)

    @pl.when(last_row)
    def _():
        bottom_in[...] = jnp.zeros_like(bottom_in)

    def count(flag):
        return jnp.where(flag, 0, 1).astype(jnp.int32)

    pl.semaphore_wait(barrier, count(first_row) + count(last_row) + count(first_col) + count(last_col) + 1)

    def copy(kind, c):
        source, target, where = {
            RIGHT: (right_off, left_in, {"cols": col + 1}),
            LEFT: (left_off, right_in, {"cols": col - 1}),
            DOWN: (down_off, top_in, {"rows": row + 1}),
            UP: (up_off, bottom_in, {"rows": row - 1}),
        }[kind]
        return pltpu.make_async_remote_copy(
            src_ref=source.at[c], dst_ref=target.at[c],
            send_sem=send_sem.at[kind, c], recv_sem=recv_sem.at[kind, c],
            device_id=where, device_id_type=pl.DeviceIdType.MESH)

    source_edge = {RIGHT: first_col, LEFT: last_col, DOWN: first_row, UP: last_row}
    sink_edge = {RIGHT: last_col, LEFT: first_col, DOWN: last_row, UP: first_row}
    several = {RIGHT: cols > 1, LEFT: cols > 1, DOWN: rows > 1, UP: rows > 1}

    def send_first(kind, c):
        if several[kind]:
            @pl.when(source_edge[kind])
            def _():
                copy(kind, c).start()

    def lanes(c):
        return pl.ds(pl.multiple_of(c * LANES, LANES), LANES)

    def relay(kind, c):
        if not several[kind]:
            return
        inside = jnp.logical_not(jnp.logical_or(source_edge[kind], sink_edge[kind]))

        @pl.when(inside)
        def _():
            copy(kind, c).wait_recv()
            rates = rates_ref[:, lanes(c)]
            if kind in (DOWN, UP):
                off, entering = (down_off, top_in) if kind == DOWN else (up_off, bottom_in)
                for j in range(nj):
                    factor = jnp.exp(rates * cs[c, pl.ds(j, 1), :])
                    off[c, j] = factor * entering[c, j] + off[c, j]
            else:
                off, entering = (right_off, left_in) if kind == RIGHT else (left_off, right_in)

                @pl.loop(0, ni)
                def _(i):
                    factor = jnp.exp(rates * jnp.sum(lt[c, i], axis=0, keepdims=True))
                    off[c, i] = factor * entering[c, i] + off[c, i]
            copy(kind, c).start()

    def take_last(kind, c):
        if several[kind]:
            @pl.when(sink_edge[kind])
            def _():
                copy(kind, c).wait_recv()

    zero = jnp.zeros((ns, LANES), F32)

    def prepare(c):
        step = steps_ref[:, lanes(c)].reshape(ni, nj, LANES)
        logs = kb[...] * step
        lt[c] = logs
        cs[c] = jnp.sum(logs, axis=0)
        dr[c] = mb[...] * step * x_ref[:, lanes(c)].astype(F32).reshape(ni, nj, LANES)
        gy[c] = gy_ref[:, lanes(c)].astype(F32).reshape(ni, nj, LANES)

    def open_ends(c):
        rates = rates_ref[:, lanes(c)]

        def body(t, cot):
            i = ni - 1 - t
            r = zero
            cot = list(cot)
            for j in range(nj):
                a = jnp.exp(rates * lt[c, i, pl.ds(j, 1), :])
                decay[c, i, j] = a
                r = a * r + im[i, j] * dr[c, i, pl.ds(j, 1), :]
                cot[j] = a * (om[i, j] * gy[c, i, pl.ds(j, 1), :] + cot[j])
            right_off[c, i] = r
            return tuple(cot)

        cot = lax.fori_loop(0, ni, body, (zero,) * nj)
        for j in range(nj):
            up_off[c, j] = cot[j]

    def forward(c):
        def body(i, state):
            r = left_in[c, i]
            state = list(state)
            for j in range(nj):
                a = decay[c, i, j]
                r = a * r + im[i, j] * dr[c, i, pl.ds(j, 1), :]
                rst[c, i, j] = r
                state[j] = a * state[j] + r
            return tuple(state)

        state = lax.fori_loop(0, ni, body, (zero,) * nj)
        for j in range(nj):
            down_off[c, j] = state[j]

    def backward(c):
        def body(t, cot):
            i = ni - 1 - t
            lead = zero
            cot = list(cot)
            for j in reversed(range(nj)):
                a = decay[c, i, j]
                here = om[i, j] * gy[c, i, pl.ds(j, 1), :] + cot[j]
                cct[c, i, j] = here
                cot[j] = a * here
                lead = cot[j] + a * lead
            left_off[c, i] = lead
            return tuple(cot)

        lax.fori_loop(0, ni, body, tuple(bottom_in[c, j] for j in range(nj)))

    def gradients(c):
        rates = rates_ref[:, lanes(c)]

        def body(i, state):
            carry = right_in[c, i]
            state = list(state)
            for j in reversed(range(nj)):
                a, here, r = decay[c, i, j], cct[c, i, j], rst[c, i, j]
                before = rst[c, i, j - 1] if j else left_in[c, i]
                kept = a * state[j]
                state[j] = kept + r
                row_cot = here + carry
                carry = a * row_cot
                change = here * kept + carry * before
                acc_out[i, j] += gy[c, i, pl.ds(j, 1), :] * state[j]
                acc_in[i, j] += dr[c, i, pl.ds(j, 1), :] * row_cot
                dc_rows[i, pl.ds(j, 1), :] = jnp.sum(row_cot * im[i, j], axis=0, keepdims=True)
                ds_rows[i, pl.ds(j, 1), :] = jnp.sum(change * rates, axis=0, keepdims=True)
            return tuple(state)

        lax.fori_loop(0, ni, body, tuple(top_in[c, j] for j in range(nj)))
        step = steps_ref[:, lanes(c)].reshape(ni, nj, LANES)
        xf = x_ref[:, lanes(c)].astype(F32).reshape(ni, nj, LANES)
        drive_cot = dc_rows[...] * mb[...]
        gx_ref[:, lanes(c)] = (drive_cot * step).reshape(patches, LANES).astype(jnp.bfloat16)
        gs_ref[:, lanes(c)] = (drive_cot * xf + kb[...] * ds_rows[...]).reshape(patches, LANES)

    @pl.loop(0, chunks)
    def _(c):
        prepare(c)
        open_ends(c)
        send_first(RIGHT, c)
        send_first(UP, c)

    acc_in[...] = jnp.zeros_like(acc_in)
    acc_out[...] = jnp.zeros_like(acc_out)

    def do_forward(c):
        relay(RIGHT, c)
        take_last(RIGHT, c)
        forward(c)
        send_first(DOWN, c)

    def do_backward(c):
        relay(UP, c)
        take_last(UP, c)
        backward(c)
        send_first(LEFT, c)

    upper = row < rows // 2

    @pl.loop(0, chunks)
    def _(c):
        @pl.when(upper)
        def _():
            do_forward(c)
            do_backward(c)

        @pl.when(jnp.logical_not(upper))
        def _():
            do_backward(c)
            do_forward(c)

        @pl.when(c > 0)
        def _():
            relay(DOWN, c - 1)

    relay(DOWN, chunks - 1)

    @pl.loop(0, chunks)
    def _(c):
        take_last(DOWN, c)
        relay(LEFT, c)
        take_last(LEFT, c)
        gradients(c)

    ones = jnp.ones((8, LANES), F32)

    def lane_sums(acc):
        return lax.dot_general(ones, acc[...].reshape(patches * ns, LANES), (((1,), (1,)), ((), ())),
                               precision=lax.Precision.HIGHEST, preferred_element_type=F32)

    which = lax.broadcasted_iota(jnp.int32, (8, patches * ns), 0)
    mine[...] = jnp.where(which == 0, lane_sums(acc_in), lane_sums(acc_out))
    swap = pltpu.make_async_remote_copy(
        src_ref=mine, dst_ref=theirs, send_sem=pair_send, recv_sem=pair_recv,
        device_id={"chan": peer}, device_id_type=pl.DeviceIdType.MESH)
    swap.start()
    for kind in (RIGHT, UP, DOWN, LEFT):
        if several[kind]:
            @pl.when(jnp.logical_not(sink_edge[kind]))
            def _():
                @pl.loop(0, chunks)
                def _(c):
                    copy(kind, c).wait_send()
    swap.wait()
    sums_ref[...] = mine[...] + theirs[...]


def local(sizes, patches, steps, decay_codes, tissue_mask, decay_rates, input_map, output_map, out_grad):
    rows, cols, chans = sizes
    ni, nj, width = steps.shape
    ns = decay_rates.shape[0]
    chunks = width // LANES
    count = ni * nj
    vmem = pl.BlockSpec(memory_space=pltpu.VMEM)

    def buf(*shape):
        return pltpu.VMEM(shape, F32)

    across = buf(chunks, ni, ns, LANES)
    along = buf(chunks, nj, ns, LANES)
    whole = buf(chunks, ni, nj, ns, LANES)
    tile = buf(ni, nj, LANES)
    tiles = buf(chunks, ni, nj, LANES)
    maps = buf(ni, nj, ns, LANES)
    gx, gs, sums = pl.pallas_call(
        functools.partial(kernel, (rows, cols, chans, ni, nj, ns, chunks)),
        out_shape=(
            jax.ShapeDtypeStruct((count, width), jnp.bfloat16),
            jax.ShapeDtypeStruct((count, width), F32),
            jax.ShapeDtypeStruct((8, count * ns), F32),
        ),
        in_specs=[vmem] * 8,
        out_specs=(vmem,) * 3,
        scratch_shapes=[
            maps, maps, tile, tile, tiles, tiles, tiles, buf(chunks, nj, LANES), whole, whole, whole,
            across, across, along, along, along, along, across, across,
            maps, maps, tile, tile, buf(8, count * ns), buf(8, count * ns),
            pltpu.SemaphoreType.DMA((4, chunks)), pltpu.SemaphoreType.DMA((4, chunks)),
            pltpu.SemaphoreType.DMA, pltpu.SemaphoreType.DMA,
        ],
        compiler_params=pltpu.CompilerParams(
            collective_id=0, has_side_effects=True, vmem_limit_bytes=44 * 1024 * 1024),
        cost_estimate=pl.CostEstimate(
            flops=40 * count * ns * width, bytes_accessed=16 * count * width,
            transcendentals=count * ns * width),
    )(patches.reshape(count, width), steps.reshape(count, width), decay_codes, tissue_mask, decay_rates,
      input_map.reshape(count, ns), output_map.reshape(count, ns), out_grad.reshape(count, width))
    shape = (ni, nj, width)
    return (gx.reshape(shape), gs.reshape(shape),
            sums[0].reshape(ni, nj, ns), sums[1].reshape(ni, nj, ns))


def solution(mesh):
    field = P(("groups", "rows"), "cols", "chan")
    plain = P(("groups", "rows"), "cols")
    proj = P(("groups", "rows"), "cols", None)
    sizes = (mesh.shape["rows"], mesh.shape["cols"], mesh.shape["chan"])
    return jax.shard_map(
        functools.partial(local, sizes), mesh=mesh,
        in_specs=(field, field, plain, plain, P(None, "chan"), proj, proj, field),
        out_specs=(field, field, proj, proj), check_vma=False)
```

time: 547 us -> 49.3 us (0.09); the launches traced: 537 us -> 48.9 us
  loops' own time: 197 us -> 0 us
  local copies, waits for them, and re-layouts: 151 us -> 8.78 us
  other arithmetic: 117 us -> 0 us
  waiting for transfers between devices: 45.8 us -> 0 us
  Pallas kernels: 0 us -> 39.5 us
  starting transfers between devices: 20.5 us -> 0 us
    another operation x10 -> x0, loops' own time: 197 us -> none  [the longest x1 31.7 us: local(): col_offset, _ = lax.scan(col_forward_last, col_zero, jnp.arange(prows))]
    dynamic_slice x112 -> x0, local copies, waits for them, and re-layouts: 66.1 us -> none  [the longest x64 38.5 us: local(): col_offset, _ = lax.scan(col_forward_last, col_zero, jnp.arange(prows))]
    ppermute x8 -> x0, waiting for transfers between devices: 45.8 us -> none  [shifted(): return lax.ppermute(block, axis, route)]
    pallas_call x0 -> x1, Pallas kernels: none -> 39.5 us  [local(): pl.pallas_call(functools.partial(kernel, (rows, cols, chans, ni, nj, ns,...]
    dynamic_update_slice x56 -> x0, local copies, waits for them, and re-layouts: 36.3 us -> none  [the longest x32 21.6 us: local(): _, (state, map_out) = lax.scan(col_forward_out, top_in, jnp.arange(prows))]
    mul x248 -> x0, local copies, waits for them, and re-layouts: 35.7 us -> none  [the longest x64 33.9 us: col_backward(): cot = output_map[i][:, :, None] * gyf[i][:, None, :] + carry]
    reduce_sum x25 -> x0, other arithmetic: 34.9 us -> none  [the longest x16 20.6 us: col_forward_out(): return (carry, (carry, jnp.sum(gyf[i][:, None, :] * carry, axis=2)))]
    mul x50 -> x0, other arithmetic: 29 us -> none  [the longest x32 17.5 us: col_backward(): return (factor * cot, cot)]
  transfers between devices with their start and end apart: 8 -> 0, of which waited for: 7 -> 0; matrix products, arithmetic and copies ran while one was open for 18% -> 0% of each run, Pallas kernels for 0% -> 0%
where the time goes in v1:
time: 49.3 us; the launch traced here: 48.9 us
  Pallas kernels  39.5 us (80%)
  local copies, waits for them, and re-layouts  8.78 us (18%)
  between operations  0.66 us (1%)
    pallas_call x1, Pallas kernels, local(): pl.pallas_call(functools.partial(kernel, (rows, cols, chans, ni, nj, ns,...  39.5 us
    unnamed x16, local copies, waits for them, and re-layouts  7.32 us

profile of v1, /device:TPU:0, one launch (start us, length us, event | category | flops | bytes accessed | tf_op | source)
XLA Modules:
  0.0 48.9 jit_solution(12245650266508859562)
XLA Ops:
  0.6 0.0 copy-start.5
  0.6 0.8 %copy.12.codes_ref = s32[16,8]{1,0:T(8,128)S(1)} copy(s32[16,8]{0,1:T(8,128)} %param.10) | data formatting | bytes 1024 | tf_op args[2]
  1.4 0.8 %copy.13.mask_ref = s32[16,8]{1,0:T(8,128)S(1)} copy(s32[16,8]{0,1:T(8,128)} %param.11) | data formatting | bytes 1024 | tf_op args[3]
  2.2 0.0 copy-done.5
  2.2 0.0 copy-start
  2.2 0.9 %copy-done = f32[16,8,512]{2,1,0:T(8,128)S(1)} copy-done((f32[16,8,512]{2,1,0:T(8,128)S(1)}, f32[16,8,512]{2,1,0:T(8,128)}, u32[]{:S(2)}) %copy-start) | copy-done | bytes 262168
  3.1 0.0 copy-start.1
  3.1 0.9 %copy-done.1 = bf16[16,8,512]{2,1,0:T(8,128)(2,1)S(1)} copy-done((bf16[16,8,512]{2,1,0:T(8,128)(2,1)S(1)}, bf16[16,8,512]{2,1,0:T(8,128)(2,1)}, u32[]{:S(2)}) %copy-start.1) | copy-done | bytes 131096
  4.0 0.0 copy-start.2
  4.0 0.9 %copy-done.2 = bf16[16,8,512]{2,1,0:T(8,128)(2,1)S(1)} copy-done((bf16[16,8,512]{2,1,0:T(8,128)(2,1)S(1)}, bf16[16,8,512]{2,1,0:T(8,128)(2,1)}, u32[]{:S(2)}) %copy-start.2) | copy-done | bytes 131096
  4.9 0.0 copy-start.3
  4.9 0.8 %copy-done.3 = f32[16,8,16]{2,1,0:T(8,128)S(1)} copy-done((f32[16,8,16]{2,1,0:T(8,128)S(1)}, f32[16,8,16]{2,1,0:T(8,128)}, u32[]{:S(2)}) %copy-start.3) | copy-done | bytes 8216
  5.8 0.0 copy-start.4
  5.8 0.8 %copy-done.4 = f32[16,8,16]{2,1,0:T(8,128)S(1)} copy-done((f32[16,8,16]{2,1,0:T(8,128)S(1)}, f32[16,8,16]{2,1,0:T(8,128)}, u32[]{:S(2)}) %copy-start.4) | copy-done | bytes 8216
  6.6 39.5 %shard_map.111 = (bf16[128,512]{1,0:T(8,128)(2,1)S(1)}, f32[128,512]{1,0:T(8,128)S(1)}, f32[8,2048]{1,0:T(8,128)S(1)}) custom-call(bf16[128,512]{1,0:T(8,128)(2,1)S(1)} %bitcast.10, f32[128,512]{1,0:T(8,128)S(1)} %bitcast.9, s32[16,8]{1,0:T(8,128)S(1)} %copy.12.codes_ref, s32[16,8]{1,0:T(8,128)S(1)} %copy.13.mask_ref, f32[16,512]{1,0:T(8,128)S(1)} %copy-done.5, ...), custom_call_target="tpu_custom_call" | custom-call | flops 41943040 | bytes 1048576 | tf_op jit(solution)/shard_map/pallas_call | solution.py:311
  46.1 0.7 %reshape_squeeze.7 = f32[16,8,16]{2,1,0:T(8,128)} reshape(f32[2048]{0:T(1024)S(1)} %get-tuple-element.10) | data formatting | bytes 16384 | tf_op jit(solution)/shard_map/reshape;squeeze | solution.py:336
  46.8 0.7 %reshape_squeeze.6 = f32[16,8,16]{2,1,0:T(8,128)} reshape(f32[2048]{0:T(1024)S(1)} %get-tuple-element.11) | data formatting | bytes 16384 | tf_op jit(solution)/shard_map/reshape;squeeze | solution.py:336
  47.5 0.7 %copy.16 = bf16[16,8,512]{2,1,0:T(8,128)(2,1)} copy(bf16[16,8,512]{2,1,0:T(8,128)(2,1)S(1)} %bitcast.8) | data formatting | bytes 262144
  48.2 0.7 %copy.17 = f32[16,8,512]{2,1,0:T(8,128)} copy(f32[16,8,512]{2,1,0:T(8,128)S(1)} %bitcast.7) | data formatting | bytes 524288
  (1 shorter events, 0.0 us)
Async XLA Ops:
  0.6 1.5 %copy-start.5 = (f32[16,512]{1,0:T(8,128)S(1)}, f32[16,512]{1,0:T(8,128)}, u32[]{:S(2)}) copy-start(f32[16,512]{1,0:T(8,128)} %rates_ref.1) | copy-start | bytes 98308
  2.2 1.0 %copy-start = (f32[16,8,512]{2,1,0:T(8,128)S(1)}, f32[16,8,512]{2,1,0:T(8,128)}, u32[]{:S(2)}) copy-start(f32[16,8,512]{2,1,0:T(8,128)} %param.9) | copy-start | bytes 786436
  3.1 0.9 %copy-start.1 = (bf16[16,8,512]{2,1,0:T(8,128)(2,1)S(1)}, bf16[16,8,512]{2,1,0:T(8,128)(2,1)}, u32[]{:S(2)}) copy-start(bf16[16,8,512]{2,1,0:T(8,128)(2,1)} %param.8) | copy-start | bytes 393220
  4.0 0.9 %copy-start.2 = (bf16[16,8,512]{2,1,0:T(8,128)(2,1)S(1)}, bf16[16,8,512]{2,1,0:T(8,128)(2,1)}, u32[]{:S(2)}) copy-start(bf16[16,8,512]{2,1,0:T(8,128)(2,1)} %param.15) | copy-start | bytes 393220
  4.9 0.8 %copy-start.3 = (f32[16,8,16]{2,1,0:T(8,128)S(1)}, f32[16,8,16]{2,1,0:T(8,128)}, u32[]{:S(2)}) copy-start(f32[16,8,16]{2,1,0:T(8,128)} %param.13) | copy-start | bytes 24580
  5.8 0.8 %copy-start.4 = (f32[16,8,16]{2,1,0:T(8,128)S(1)}, f32[16,8,16]{2,1,0:T(8,128)}, u32[]{:S(2)}) copy-start(f32[16,8,16]{2,1,0:T(8,128)} %param.14) | copy-start | bytes 24580

commit v2 on v1

--- a/solution.py
+++ b/solution.py
@@ -13,8 +13,9 @@
 RIGHT, DOWN, UP, LEFT = range(4)
 
 
-def kernel(dims, x_ref, steps_ref, codes_ref, mask_ref, rates_ref, imap_ref, omap_ref, gy_ref,
-           gx_ref, gs_ref, sums_ref,
+def kernel(dims, x_hbm, steps_hbm, codes_hbm, mask_hbm, rates_hbm, imap_hbm, omap_hbm, gy_hbm,
+           gx_ref, gs_ref, gi_ref, go_ref,
+           x_ref, steps_ref, codes_ref, mask_ref, rates_ref, imap_ref, omap_ref, gy_ref, load_sem,
            im, om, kb, mb, lt, dr, gy, cs, decay, rst, cct,
            right_off, left_in, down_off, top_in, up_off, bottom_in, left_off, right_in,
            acc_in, acc_out, dc_rows, ds_rows, mine, theirs,
@@ -25,6 +26,12 @@
     first_row, last_row = row == 0, row == rows - 1
     first_col, last_col = col == 0, col == cols - 1
 
+    loads = [pltpu.make_async_copy(source, target, load_sem.at[k]) for k, (source, target) in enumerate((
+        (codes_hbm, codes_ref), (mask_hbm, mask_ref), (imap_hbm, imap_ref), (omap_hbm, omap_ref),
+        (rates_hbm, rates_ref), (steps_hbm, steps_ref), (x_hbm, x_ref), (gy_hbm, gy_ref)))]
+    for load in loads:
+        load.start()
+
     barrier = pltpu.get_barrier_semaphore()
 
     def greet(there, target):
@@ -46,9 +53,10 @@
         return lax.dot_general(one, value, (((1,), (1,)), ((), ())),
                                precision=lax.Precision.HIGHEST, preferred_element_type=F32)
 
-    maskf = mask_ref[...].astype(F32)
-    keep = maskf * jnp.log(0.7 + 0.25 * codes_ref[...].astype(F32) / (CODES - 1))
-    keep_t, mask_t = turned(keep, nj), turned(maskf, nj)
+    for load in loads[:4]:
+        load.wait()
+    mask_t = mask_ref[...].astype(F32)
+    keep_t = mask_t * jnp.log(0.7 + 0.25 * codes_ref[...].astype(F32) / (CODES - 1))
     for i in range(ni):
         kb[i] = jnp.broadcast_to(keep_t[:, i:i + 1], (nj, LANES))
         mb[i] = jnp.broadcast_to(mask_t[:, i:i + 1], (nj, LANES))
@@ -56,6 +64,9 @@
     for p in range(patches):
         im[p // nj, p % nj] = jnp.broadcast_to(im_t[:, p:p + 1], (ns, LANES))
         om[p // nj, p % nj] = jnp.broadcast_to(om_t[:, p:p + 1], (ns, LANES))
+
+    for load in loads[4:]:
+        load.wait()
 
     @pl.when(first_col)
     def _():
@@ -142,11 +153,23 @@
         dr[c] = mb[...] * step * x_ref[:, lanes(c)].astype(F32).reshape(ni, nj, LANES)
         gy[c] = gy_ref[:, lanes(c)].astype(F32).reshape(ni, nj, LANES)
 
+    group = 2 if ni % 2 == 0 else 1
+
+    def down_rows(body, carry):
+        def several_rows(t, carry):
+            for k in range(group):
+                carry = body(t * group + k, carry)
+            return carry
+
+        return lax.fori_loop(0, ni // group, several_rows, carry)
+
+    def up_rows(body, carry):
+        return down_rows(lambda t, value: body(ni - 1 - t, value), carry)
+
     def open_ends(c):
         rates = rates_ref[:, lanes(c)]
 
-        def body(t, cot):
-            i = ni - 1 - t
+        def body(i, cot):
             r = zero
             cot = list(cot)
             for j in range(nj):
@@ -157,7 +180,7 @@
             right_off[c, i] = r
             return tuple(cot)
 
-        cot = lax.fori_loop(0, ni, body, (zero,) * nj)
+        cot = up_rows(body, (zero,) * nj)
         for j in range(nj):
             up_off[c, j] = cot[j]
 
@@ -172,13 +195,12 @@
                 state[j] = a * state[j] + r
             return tuple(state)
 
-        state = lax.fori_loop(0, ni, body, (zero,) * nj)
+        state = down_rows(body, (zero,) * nj)
         for j in range(nj):
             down_off[c, j] = state[j]
 
     def backward(c):
-        def body(t, cot):
-            i = ni - 1 - t
+        def body(i, cot):
             lead = zero
             cot = list(cot)
             for j in reversed(range(nj)):
@@ -190,7 +212,7 @@
             left_off[c, i] = lead
             return tuple(cot)
 
-        lax.fori_loop(0, ni, body, tuple(bottom_in[c, j] for j in range(nj)))
+        up_rows(body, tuple(bottom_in[c, j] for j in range(nj)))
 
     def gradients(c):
         rates = rates_ref[:, lanes(c)]
@@ -212,7 +234,7 @@
                 ds_rows[i, pl.ds(j, 1), :] = jnp.sum(change * rates, axis=0, keepdims=True)
             return tuple(state)
 
-        lax.fori_loop(0, ni, body, tuple(top_in[c, j] for j in range(nj)))
+        down_rows(body, tuple(top_in[c, j] for j in range(nj)))
         step = steps_ref[:, lanes(c)].reshape(ni, nj, LANES)
         xf = x_ref[:, lanes(c)].astype(F32).reshape(ni, nj, LANES)
         drive_cot = dc_rows[...] * mb[...]
@@ -236,7 +258,6 @@
         send_first(DOWN, c)
 
     def do_backward(c):
-        relay(UP, c)
         take_last(UP, c)
         backward(c)
         send_first(LEFT, c)
@@ -245,6 +266,8 @@
 
     @pl.loop(0, chunks)
     def _(c):
+        relay(UP, c)
+
         @pl.when(upper)
         def _():
             do_forward(c)
@@ -268,14 +291,22 @@
         take_last(LEFT, c)
         gradients(c)
 
-    ones = jnp.ones((8, LANES), F32)
+    ones = jnp.ones((8, LANES), jnp.bfloat16)
 
     def lane_sums(acc):
-        return lax.dot_general(ones, acc[...].reshape(patches * ns, LANES), (((1,), (1,)), ((), ())),
-                               precision=lax.Precision.HIGHEST, preferred_element_type=F32)
-
-    which = lax.broadcasted_iota(jnp.int32, (8, patches * ns), 0)
-    mine[...] = jnp.where(which == 0, lane_sums(acc_in), lane_sums(acc_out))
+        whole = acc[...].reshape(patches * ns, LANES)
+        high = whole.astype(jnp.bfloat16)
+        low = (whole - high.astype(F32)).astype(jnp.bfloat16)
+
+        def dot(part):
+            return lax.dot_general(ones, part, (((1,), (1,)), ((), ())), preferred_element_type=F32)
+
+        return dot(high) + dot(low)
+
+    for which, acc in enumerate((acc_in, acc_out)):
+        flat = lane_sums(acc)
+        for i in range(ni):
+            mine[which, pl.ds(i, 1), :] = flat[0:1, i * nj * ns:(i + 1) * nj * ns]
     swap = pltpu.make_async_remote_copy(
         src_ref=mine, dst_ref=theirs, send_sem=pair_send, recv_sem=pair_recv,
         device_id={"chan": peer}, device_id_type=pl.DeviceIdType.MESH)
@@ -288,7 +319,20 @@
                 def _(c):
                     copy(kind, c).wait_send()
     swap.wait()
-    sums_ref[...] = mine[...] + theirs[...]
+    for which, target in enumerate((gi_ref, go_ref)):
+        total = mine[which] + theirs[which]
+        for j in range(nj):
+            target[:, j, :] = total[:, j * ns:(j + 1) * ns]
+
+
+def finish(*refs):
+    half = (len(refs) - 1) // 2
+    sem = refs[-1]
+    stores = [pltpu.make_async_copy(refs[k], refs[half + k], sem.at[k]) for k in range(half)]
+    for store in stores:
+        store.start()
+    for store in stores:
+        store.wait()
 
 
 def local(sizes, patches, steps, decay_codes, tissue_mask, decay_rates, input_map, output_map, out_grad):
@@ -298,6 +342,7 @@
     chunks = width // LANES
     count = ni * nj
     vmem = pl.BlockSpec(memory_space=pltpu.VMEM)
+    hbm = pl.BlockSpec(memory_space=pltpu.HBM)
 
     def buf(*shape):
         return pltpu.VMEM(shape, F32)
@@ -308,32 +353,42 @@
     tile = buf(ni, nj, LANES)
     tiles = buf(chunks, ni, nj, LANES)
     maps = buf(ni, nj, ns, LANES)
-    gx, gs, sums = pl.pallas_call(
+    results = pl.pallas_call(
         functools.partial(kernel, (rows, cols, chans, ni, nj, ns, chunks)),
         out_shape=(
             jax.ShapeDtypeStruct((count, width), jnp.bfloat16),
             jax.ShapeDtypeStruct((count, width), F32),
-            jax.ShapeDtypeStruct((8, count * ns), F32),
+            jax.ShapeDtypeStruct((ni, nj, ns), F32),
+            jax.ShapeDtypeStruct((ni, nj, ns), F32),
         ),
-        in_specs=[vmem] * 8,
-        out_specs=(vmem,) * 3,
+        in_specs=[hbm] * 8,
+        out_specs=(vmem,) * 4,
         scratch_shapes=[
+            pltpu.VMEM((count, width), jnp.bfloat16), buf(count, width), pltpu.VMEM((nj, ni), jnp.int32),
+            pltpu.VMEM((nj, ni), jnp.int32), buf(ns, width), buf(count, ns), buf(count, ns),
+            pltpu.VMEM((count, width), jnp.bfloat16), pltpu.SemaphoreType.DMA((8,)),
             maps, maps, tile, tile, tiles, tiles, tiles, buf(chunks, nj, LANES), whole, whole, whole,
             across, across, along, along, along, along, across, across,
-            maps, maps, tile, tile, buf(8, count * ns), buf(8, count * ns),
+            maps, maps, tile, tile, buf(2, ni, nj * ns), buf(2, ni, nj * ns),
             pltpu.SemaphoreType.DMA((4, chunks)), pltpu.SemaphoreType.DMA((4, chunks)),
             pltpu.SemaphoreType.DMA, pltpu.SemaphoreType.DMA,
         ],
         compiler_params=pltpu.CompilerParams(
-            collective_id=0, has_side_effects=True, vmem_limit_bytes=44 * 1024 * 1024),
+            collective_id=0, has_side_effects=True, vmem_limit_bytes=63 * 1024 * 1024),
         cost_estimate=pl.CostEstimate(
             flops=40 * count * ns * width, bytes_accessed=16 * count * width,
             transcendentals=count * ns * width),
-    )(patches.reshape(count, width), steps.reshape(count, width), decay_codes, tissue_mask, decay_rates,
+    )(patches.reshape(count, width), steps.reshape(count, width), decay_codes.T, tissue_mask.T, decay_rates,
       input_map.reshape(count, ns), output_map.reshape(count, ns), out_grad.reshape(count, width))
+    gx, gs, gi, go = pl.pallas_call(
+        finish,
+        out_shape=tuple(jax.ShapeDtypeStruct(value.shape, value.dtype) for value in results),
+        in_specs=[pl.BlockSpec(memory_space=pl.ANY)] * 4,
+        out_specs=(hbm,) * 4,
+        scratch_shapes=[pltpu.SemaphoreType.DMA((4,))],
+    )(*results)
     shape = (ni, nj, width)
-    return (gx.reshape(shape), gs.reshape(shape),
-            sums[0].reshape(ni, nj, ns), sums[1].reshape(ni, nj, ns))
+    return gx.reshape(shape), gs.reshape(shape), gi, go
 
 
 def solution(mesh):

time: 49.3 us -> 58 us (1.18)
  Pallas kernels: 39.5 us -> 57.2 us
  local copies, waits for them, and re-layouts: 8.78 us -> 0 us
    pallas_call x0 -> x1, Pallas kernels: none -> 17 us  [local(): pl.pallas_call(finish, out_shape=tuple((jax.ShapeDtypeStruct(value.shape,...]
    unnamed x16 -> x0, local copies, waits for them, and re-layouts: 7.32 us -> none
    another operation x2 -> x0, local copies, waits for them, and re-layouts: 1.42 us -> none  [the longest x1 0.71 us: local(): sums[1].reshape(ni, nj, ns)]
    pallas_call x1, Pallas kernels: 39.5 us -> 40.1 us  [local(): pl.pallas_call(functools.partial(kernel, (rows, cols, chans, ni, nj, ns,...]
where the time goes in v2:
time: 58 us; the launch traced here: 57.8 us
  Pallas kernels  57.2 us (99%)
  between operations  0.64 us (1%)
    pallas_call x1, Pallas kernels, local(): pl.pallas_call(functools.partial(kernel, (rows, cols, chans, ni, nj, ns,...  40.1 us
    pallas_call x1, Pallas kernels, local(): pl.pallas_call(finish, out_shape=tuple((jax.ShapeDtypeStruct(value.shape,...  17 us

profile of v2, /device:TPU:0, one launch (start us, length us, event | category | flops | bytes accessed | tf_op | source)
XLA Modules:
  0.0 57.8 jit_solution(15774907089136922295)
XLA Ops:
  0.6 40.1 %shard_map.111 = (bf16[128,512]{1,0:T(8,128)(2,1)}, f32[128,512]{1,0:T(8,128)}, f32[16,8,16]{2,1,0:T(8,128)}, f32[16,8,16]{2,1,0:T(8,128)}) custom-call(bf16[128,512]{1,0:T(8,128)(2,1)} %bitcast.11, f32[128,512]{1,0:T(8,128)} %bitcast.9, s32[8,16]{1,0:T(8,128)} %bitcast.16, s32[8,16]{1,0:T(8,128)} %bitcast.17, f32[16,512]{1,0:T(8,128)} %rates_hbm.1, ...), custom_call_target="tpu_custom_call" | custom-call | flops 41943040 | bytes 1048576 | tf_op jit(solution)/shard_map/pallas_call | solution.py:356
  40.8 17.0 %shard_map.112 = (bf16[128,512]{1,0:T(8,128)(2,1)}, f32[128,512]{1,0:T(8,128)}, f32[16,8,16]{2,1,0:T(8,128)}, f32[16,8,16]{2,1,0:T(8,128)}) custom-call(bf16[128,512]{1,0:T(8,128)(2,1)} %get-tuple-element.12.refs_0_, f32[128,512]{1,0:T(8,128)} %get-tuple-element.13.refs_1_, f32[16,8,16]{2,1,0:T(8,128)} %get-tuple-element.14.refs_2_, ...), custom_call_target="tpu_custom_call" | custom-call | tf_op jit(solution)/shard_map/pallas_call | solution.py:383

commit v3 on v2

--- a/solution.py
+++ b/solution.py
@@ -214,12 +214,26 @@
 
         up_rows(body, tuple(bottom_in[c, j] for j in range(nj)))
 
+    row_of = lax.broadcasted_iota(jnp.int32, (8, LANES), 0)
+
+    def state_sums(terms):
+        if nj != 8 or ns % 8:
+            return jnp.concatenate([jnp.sum(term, axis=0, keepdims=True) for term in terms], axis=0)
+        level = [sum(term[k:k + 8] for k in range(0, ns, 8)) for term in terms]
+        for reach in (1, 2, 4):
+            even = (row_of & reach) == 0
+            level = [jnp.where(even, first, second)
+                     + pltpu.roll(jnp.where(even, second, first), 8 - reach, 0)
+                     for first, second in zip(level[0::2], level[1::2])]
+        return level[0]
+
     def gradients(c):
         rates = rates_ref[:, lanes(c)]
 
         def body(i, state):
             carry = right_in[c, i]
             state = list(state)
+            drive_terms, step_terms = [None] * nj, [None] * nj
             for j in reversed(range(nj)):
                 a, here, r = decay[c, i, j], cct[c, i, j], rst[c, i, j]
                 before = rst[c, i, j - 1] if j else left_in[c, i]
@@ -230,8 +244,10 @@
                 change = here * kept + carry * before
                 acc_out[i, j] += gy[c, i, pl.ds(j, 1), :] * state[j]
                 acc_in[i, j] += dr[c, i, pl.ds(j, 1), :] * row_cot
-                dc_rows[i, pl.ds(j, 1), :] = jnp.sum(row_cot * im[i, j], axis=0, keepdims=True)
-                ds_rows[i, pl.ds(j, 1), :] = jnp.sum(change * rates, axis=0, keepdims=True)
+                drive_terms[j] = row_cot * im[i, j]
+                step_terms[j] = change * rates
+            dc_rows[i] = state_sums(drive_terms)
+            ds_rows[i] = state_sums(step_terms)
             return tuple(state)
 
         down_rows(body, tuple(top_in[c, j] for j in range(nj)))
@@ -245,8 +261,12 @@
     def _(c):
         prepare(c)
         open_ends(c)
+        send_first(UP, c)
         send_first(RIGHT, c)
-        send_first(UP, c)
+
+    @pl.loop(0, chunks)
+    def _(c):
+        relay(UP, c)
 
     acc_in[...] = jnp.zeros_like(acc_in)
     acc_out[...] = jnp.zeros_like(acc_out)
@@ -266,8 +286,6 @@
 
     @pl.loop(0, chunks)
     def _(c):
-        relay(UP, c)
-
         @pl.when(upper)
         def _():
             do_forward(c)
@@ -326,10 +344,15 @@
 
 
 def finish(*refs):
-    half = (len(refs) - 1) // 2
-    sem = refs[-1]
-    stores = [pltpu.make_async_copy(refs[k], refs[half + k], sem.at[k]) for k in range(half)]
-    for store in stores:
+    arrays = (len(refs) - 2) // 3
+    sources, targets, held = refs[:arrays], refs[arrays:2 * arrays], refs[2 * arrays:3 * arrays]
+    load_sem, store_sem = refs[3 * arrays:]
+    loads = [pltpu.make_async_copy(sources[k], held[k], load_sem.at[k]) for k in range(arrays)]
+    stores = [pltpu.make_async_copy(held[k], targets[k], store_sem.at[k]) for k in range(arrays)]
+    for load in loads:
+        load.start()
+    for load, store in zip(loads, stores):
+        load.wait()
         store.start()
     for store in stores:
         store.wait()
@@ -383,9 +406,11 @@
     gx, gs, gi, go = pl.pallas_call(
         finish,
         out_shape=tuple(jax.ShapeDtypeStruct(value.shape, value.dtype) for value in results),
-        in_specs=[pl.BlockSpec(memory_space=pl.ANY)] * 4,
+        in_specs=[hbm] * 4,
         out_specs=(hbm,) * 4,
-        scratch_shapes=[pltpu.SemaphoreType.DMA((4,))],
+        scratch_shapes=[pltpu.VMEM(value.shape, value.dtype) for value in results]
+        + [pltpu.SemaphoreType.DMA((4,))] * 2,
+        compiler_params=pltpu.CompilerParams(vmem_limit_bytes=63 * 1024 * 1024),
     )(*results)
     shape = (ni, nj, width)
     return gx.reshape(shape), gs.reshape(shape), gi, go

time: 58 us -> 34.3 us (0.59)
  Pallas kernels: 57.2 us -> 33.5 us
    pallas_call x1, Pallas kernels: 17 us -> 1.83 us  [local(): pl.pallas_call(finish, out_shape=tuple((jax.ShapeDtypeStruct(value.shape,...]
    pallas_call x1, Pallas kernels: 40.1 us -> 31.6 us  [local(): pl.pallas_call(functools.partial(kernel, (rows, cols, chans, ni, nj, ns,...]
where the time goes in v3:
time: 34.3 us; the launch traced here: 34.1 us
  Pallas kernels  33.5 us (98%)
  between operations  0.64 us (2%)
    pallas_call x1, Pallas kernels, local(): pl.pallas_call(functools.partial(kernel, (rows, cols, chans, ni, nj, ns,...  31.6 us
    pallas_call x1, Pallas kernels, local(): pl.pallas_call(finish, out_shape=tuple((jax.ShapeDtypeStruct(value.shape,...  1.83 us

profile of v3, /device:TPU:0, one launch (start us, length us, event | category | flops | bytes accessed | tf_op | source)
XLA Modules:
  0.0 34.1 jit_solution(17265698279420834906)
XLA Ops:
  0.6 31.6 %shard_map.111 = (bf16[128,512]{1,0:T(8,128)(2,1)}, f32[128,512]{1,0:T(8,128)}, f32[16,8,16]{2,1,0:T(8,128)}, f32[16,8,16]{2,1,0:T(8,128)}) custom-call(bf16[128,512]{1,0:T(8,128)(2,1)} %bitcast.11, f32[128,512]{1,0:T(8,128)} %bitcast.9, s32[8,16]{1,0:T(8,128)} %bitcast.16, s32[8,16]{1,0:T(8,128)} %bitcast.17, f32[16,512]{1,0:T(8,128)} %rates_hbm.1, ...), custom_call_target="tpu_custom_call" | custom-call | flops 41943040 | bytes 1048576 | tf_op jit(solution)/shard_map/pallas_call | solution.py:379
  32.3 1.8 %shard_map.112 = (bf16[128,512]{1,0:T(8,128)(2,1)}, f32[128,512]{1,0:T(8,128)}, f32[16,8,16]{2,1,0:T(8,128)}, f32[16,8,16]{2,1,0:T(8,128)}) custom-call(bf16[128,512]{1,0:T(8,128)(2,1)} %get-tuple-element.12.refs_0_, f32[128,512]{1,0:T(8,128)} %get-tuple-element.13.refs_1_, f32[16,8,16]{2,1,0:T(8,128)} %get-tuple-element.14.refs_2_, ...), custom_call_target="tpu_custom_call" | custom-call | tf_op jit(solution)/shard_map/pallas_call | solution.py:406
